TPU v7x, 128 devices: a whole 4x4x4 slice. The times are simulated.
128 devices in a mesh: lat: 8 (over x_hi, y), lon: 16 (over z, x_lo, core).
Axes of the slice: x: 4 (x_hi: 2, x_lo: 2; x = x_hi * 2 + x_lo), y: 4, z: 4, core: 2. Of those that a mesh axis runs over, the one named last changes fastest.
Arguments:
- tokens: float32 [4, 192, 384, 512], P(None, 'lat', 'lon'), may hold values from -6 to 6
- region: int32 [4, 192, 384], P(None, 'lat', 'lon'), may hold values from 0 to 2
- rel_index: int32 [144, 144], replicated, may hold values from 0 to 758
- rel_table: float32 [8, 759], replicated, may hold values from -5 to 5
- norm1_gain: float32 [512], replicated, may hold values from 0.1 to 1.9
- norm1_bias: float32 [512], replicated, may hold values from -3 to 3
- qkv_weight: bfloat16 [512, 1536], replicated, may hold values from -2.2 to 2.2
- qkv_bias: float32 [1536], replicated, may hold values from -3 to 3
- proj_weight: bfloat16 [512, 512], replicated, may hold values from -0.25 to 0.25
- proj_bias: float32 [512], replicated, may hold values from -3 to 3
- norm2_gain: float32 [512], replicated, may hold values from 0.1 to 1.9
- norm2_bias: float32 [512], replicated, may hold values from -3 to 3
- fc1_weight: bfloat16 [512, 2048], replicated, may hold values from -0.25 to 0.25
- fc1_bias: float32 [2048], replicated, may hold values from -3 to 3
- fc2_weight: bfloat16 [2048, 512], replicated, may hold values from -0.125 to 0.125
- fc2_bias: float32 [512], replicated, may hold values from -3 to 3
- merge_gain: float32 [2048], replicated, may hold values from 0.1 to 1.9
- merge_bias: float32 [2048], replicated, may hold values from -3 to 3
- merge_weight: bfloat16 [2048, 1024], replicated, may hold values from -0.125 to 0.125
Outputs:
- merged: bfloat16 [4, 96, 192, 1024], P(None, 'lat', 'lon')
All inputs are finite; a program needn't handle non-finite values.
Results may differ from a plain program's by a relative error of at most 0.012.
The roundings to bfloat16 on the way count: a program that leaves them out, or rounds other values in their place, can miss the bound.
Values sent between devices are 32-bit elements; how exact they have to be, the bound alone decides.
A program may use at most 192 MiB of HBM per device.

v0:
```python
import jax
import jax.numpy as jnp
from jax import lax
from jax.sharding import PartitionSpec as P

WL = 2
WH = 6
WW = 12


EPS = 1e-05


def shifted(value, axis, steps):
    count = lax.axis_size(axis)
    pairs = [(source, (source + steps) % count) for source in range(count)]
    return lax.ppermute(value, axis, pairs)


def layer_norm(values, norm_gain, norm_bias):
    centre_val = jnp.mean(values, -1, keepdims=True)
    centred = values - centre_val
    variance = jnp.mean(centred * centred, -1, keepdims=True)
    return centred * lax.rsqrt(variance + EPS) * norm_gain + norm_bias


def rotate_levels(field):
    return jnp.concatenate([field[1:], field[:1]], 0)


def assemble(upper_left, upper_right, lower_left, lower_right):
    upper = jnp.concatenate([upper_left, upper_right], 2)
    lower = jnp.concatenate([lower_left, lower_right], 2)
    return jnp.concatenate([upper, lower], 1)


def windows_of(field):
    lev_count, row_count, col_count = field.shape[:3]
    trailing = field.shape[3:]
    blocks = field.reshape(
        (lev_count // WL, WL, row_count // WH, WH, col_count // WW, WW) + trailing
    )
    order_axes = (2, 4, 0, 1, 3, 5) + tuple(range(6, 6 + len(trailing)))
    return blocks.transpose(order_axes).reshape((-1, WL * WH * WW) + trailing)


def frame_of(wins, lev_count, row_count, col_count):
    trailing = wins.shape[2:]
    blocks = wins.reshape(
        (row_count // WH, col_count // WW, lev_count // WL, WL, WH, WW) + trailing
    )
    order_axes = (2, 3, 0, 4, 1, 5) + tuple(range(6, 6 + len(trailing)))
    return blocks.transpose(order_axes).reshape((lev_count, row_count, col_count) + trailing)


def window_block(wins, region_ids, band_ids, pair_bias, params):
    (
        norm1_gain,
        norm1_bias,
        qkv_weight,
        qkv_bias,
        proj_weight,
        proj_bias,
        norm2_gain,
        norm2_bias,
        fc1_weight,
        fc1_bias,
        fc2_weight,
        fc2_bias,
    ) = params
    win_count, win_tokens, width = wins.shape
    num_heads = pair_bias.shape[0]
    head_size = width // num_heads
    tokens_flat = wins.reshape(win_count * win_tokens, width)
    normed1 = layer_norm(tokens_flat, norm1_gain, norm1_bias).astype(jnp.bfloat16)
    packed = (jnp.dot(normed1, qkv_weight, preferred_element_type=jnp.float32) + qkv_bias).astype(
        jnp.bfloat16
    )
    packed = packed.reshape(win_count, win_tokens, 3, num_heads, head_size)
    queries = packed[:, :, 0]
    key_heads = packed[:, :, 1]
    values = packed[:, :, 2]
    scores = jnp.einsum(
        "nahd,nbhd->nhab", queries, key_heads, preferred_element_type=jnp.float32
    ) * head_size ** (-0.5)
    scores = scores + pair_bias[None]
    allowed = (region_ids[:, :, None] == region_ids[:, None, :]) & (
        band_ids[:, :, None] == band_ids[:, None, :]
    )
    scores = jnp.where(allowed[:, None], scores, jnp.float32(-1e30))
    row_max = jnp.max(scores, -1, keepdims=True)
    powers = jnp.exp(scores - row_max)
    weights = (powers / jnp.sum(powers, -1, keepdims=True)).astype(jnp.bfloat16)
    attended = jnp.einsum(
        "nhab,nbhd->nahd", weights, values, preferred_element_type=jnp.float32
    ).astype(jnp.bfloat16)
    attended = attended.reshape(win_count * win_tokens, width)
    hidden = (
        jnp.dot(attended, proj_weight, preferred_element_type=jnp.float32) + proj_bias + tokens_flat
    )
    normed2 = layer_norm(hidden, norm2_gain, norm2_bias).astype(jnp.bfloat16)
    activated = jax.nn.gelu(
        jnp.dot(normed2, fc1_weight, preferred_element_type=jnp.float32) + fc1_bias,
        approximate=False,
    ).astype(jnp.bfloat16)
    result = jnp.dot(activated, fc2_weight, preferred_element_type=jnp.float32) + fc2_bias + hidden
    return result.reshape(win_count, win_tokens, width)


def merge_patches(field, merge_gain, merge_bias, merge_weight):
    lev_count, row_count, col_count, width = field.shape
    grouped = field.reshape(lev_count, row_count // 2, 2, col_count // 2, 2, width)
    grouped = grouped.transpose(0, 1, 3, 4, 2, 5).reshape(
        lev_count, row_count // 2, col_count // 2, 4 * width
    )
    normed3 = layer_norm(grouped, merge_gain, merge_bias).astype(jnp.bfloat16)
    product = jnp.dot(
        normed3.reshape(-1, 4 * width), merge_weight, preferred_element_type=jnp.float32
    )
    return product.astype(jnp.bfloat16).reshape(lev_count, row_count // 2, col_count // 2, -1)


def run_windows(field, field_ids, field_bands, pair_bias, params):
    lev_count, row_count, col_count = field_ids.shape
    result = window_block(
        windows_of(rotate_levels(field)),
        windows_of(rotate_levels(field_ids)),
        windows_of(field_bands),
        pair_bias,
        params,
    )
    return frame_of(result, lev_count, row_count, col_count)


def per_device(
    tokens,
    region,
    rel_index,
    rel_table,
    norm1_gain,
    norm1_bias,
    qkv_weight,
    qkv_bias,
    proj_weight,
    proj_bias,
    norm2_gain,
    norm2_bias,
    fc1_weight,
    fc1_bias,
    fc2_weight,
    fc2_bias,
    merge_gain,
    merge_bias,
    merge_weight,
):
    params = (
        norm1_gain,
        norm1_bias,
        qkv_weight,
        qkv_bias,
        proj_weight,
        proj_bias,
        norm2_gain,
        norm2_bias,
        fc1_weight,
        fc1_bias,
        fc2_weight,
        fc2_bias,
    )
    pair_bias = rel_table[:, rel_index]
    lev_count, row_count, col_count, width = tokens.shape
    half_rows = WH // 2
    half_cols = WW // 2
    lat_total = row_count * lax.axis_size("lat")
    first_row = lax.axis_index("lat") * row_count - half_rows
    row_orig = first_row + jnp.arange(row_count, dtype=jnp.int32)
    wrapped = jnp.mod(row_orig, lat_total)
    lat_band = (wrapped >= lat_total - half_rows).astype(jnp.int32)
    lev_band = (jnp.arange(lev_count, dtype=jnp.int32) == lev_count - 1).astype(jnp.int32)
    band_ids = jnp.broadcast_to(lev_band[:, None, None] * 2 + lat_band[None, :, None], region.shape)
    tail_tokens, tail_ids = shifted(
        (tokens[:, :, col_count - half_cols :], region[:, :, col_count - half_cols :]), "lon", 1
    )
    corner_tokens, upper_tokens, corner_ids, upper_ids = shifted(
        (
            tail_tokens[:, row_count - half_rows :],
            tokens[:, row_count - half_rows :, : col_count - half_cols],
            tail_ids[:, row_count - half_rows :],
            region[:, row_count - half_rows :, : col_count - half_cols],
        ),
        "lat",
        1,
    )
    wide = assemble(
        corner_tokens,
        upper_tokens,
        tail_tokens[:, : row_count - half_rows],
        tokens[:, : row_count - half_rows, : col_count - half_cols],
    )
    wide_ids = assemble(
        corner_ids,
        upper_ids,
        tail_ids[:, : row_count - half_rows],
        region[:, : row_count - half_rows, : col_count - half_cols],
    )
    block_out = run_windows(wide, wide_ids, band_ids, pair_bias, params)
    below = shifted(block_out[:, :half_rows], "lat", -1)
    beside_upper, beside_lower = shifted(
        (block_out[:, half_rows:, :half_cols], below[:, :, :half_cols]), "lon", -1
    )
    settled = assemble(
        block_out[:, half_rows:, half_cols:], beside_upper, below[:, :, half_cols:], beside_lower
    )
    restored = jnp.concatenate([settled[lev_count - 1 :], settled[: lev_count - 1]], 0)
    return merge_patches(restored, merge_gain, merge_bias, merge_weight)


def solution(mesh):
    return jax.shard_map(
        per_device,
        mesh=mesh,
        in_specs=(
            P(None, "lat", "lon", None),
            P(None, "lat", "lon"),
            P(),
            P(),
            P(),
            P(),
            P(),
            P(),
            P(),
            P(),
            P(),
            P(),
            P(),
            P(),
            P(),
            P(),
            P(),
            P(),
            P(),
        ),
        out_specs=P(None, "lat", "lon", None),
        check_vma=False,
    )
```

profile of v0, /device:TPU:59, one launch (start us, length us, event | category | flops | bytes accessed | tf_op | source)
XLA Modules:
  0.0 410.1 jit_solution(5481802323958689757)
XLA Ops:
  19.6 38.9 %gather_fusion = f32[20736,8]{1,0:T(8,128)} fusion(f32[8,759]{0,1:T(8,128)S(1)} %copy.77, s32[21504]{0:T(1024)S(1)} %pad_clamp_fusion), kind=kCustom, calls=%fused_computation | custom fusion | bytes 1410048 | tf_op jit(solution)/shard_map/gather | solution.py:170
  58.5 11.7 %copy.78 = f32[144,144,8]{0,1,2:T(8,128)} copy(f32[144,144,8]{2,1,0:T(8,128)} %bitcast.60) | data formatting | bytes 1327104 | tf_op jit(solution)/shard_map/gather | solution.py:170
  90.0 7.2 %reshape.172 = f32[2,2,4,6,2,12,512]{6,1,0,5,4,3,2:T(2,128)} reshape(f32[4,24,24,512]{3,0,2,1:T(4,128)} %copy.65) | data formatting | bytes 9437184 | tf_op jit(solution)/shard_map/reshape | solution.py:40
  109.7 6.5 %copy.66 = f32[4,2,2,2,6,12,512]{6,5,4,3,2,1,0:T(8,128)} copy(f32[4,2,2,2,6,12,512]{6,3,2,5,1,4,0:T(2,128)} %bitcast.57) | data formatting | bytes 9437184 | tf_op jit(solution)/shard_map/transpose | solution.py:44
  116.2 6.7 %reshape_reshape.6 = f32[2304,512]{1,0:T(8,128)} reshape(f32[4,2,2,2,6,12,512]{6,5,4,3,2,1,0:T(8,128)} %copy.66) | data formatting | bytes 9437184 | tf_op jit(solution)/shard_map/reshape;reshape | solution.py:74
  122.9 8.5 %add_convert_fusion = bf16[2304,1536]{1,0:T(8,128)(2,1)} fusion(bf16[512,1536]{1,0:T(8,128)(2,1)} %param.25, f32[1536]{0:T(1024)S(1)} %copy-done.13, f32[2304,512]{1,0:T(8,128)} %reshape_reshape.6, f32[512]{0:T(512)S(1)} %copy-done.17, f32[512]{0:T(512)S(1)} %copy-done.18, f32[2304]{0:T(1024)S(1)} %rsqrt.31, f32[2304]{0:T(1024)S(1)} %div.31), kind=kOutput, calls=%fused_computation.24 | convolution fusion | flops 3636854784 | bytes 13398016 | tf_op jit(solution)/shard_map/dot_general | solution.py:76
  131.5 18.0 %reshape.190 = bf16[16,144,3,8,64]{4,3,2,1,0:T(8,128)(2,1)} reshape(bf16[2304,1536]{1,0:T(8,128)(2,1)} %add_convert_fusion) | data formatting | bytes 14155776 | tf_op jit(solution)/shard_map/reshape | solution.py:79
  149.5 13.1 %fusion.119 = (bf16[16,144,1,8,64]{4,3,2,1,0:T(8,128)(2,1)}, bf16[16,144,1,8,64]{4,3,2,1,0:T(8,128)(2,1)}, bf16[16,144,1,8,64]{4,3,2,1,0:T(8,128)(2,1)}) fusion(bf16[16,144,3,8,64]{4,3,2,1,0:T(8,128)(2,1)} %reshape.190), kind=kLoop, calls=%fused_computation.162 | loop fusion | bytes 14155776 | tf_op jit(solution)/shard_map/slice | solution.py:82
  162.6 7.8 %copy.88 = bf16[16,144,1,8,64]{1,4,3,0,2:T(8,128)(2,1)} copy(bf16[16,144,1,8,64]{4,3,2,1,0:T(8,128)(2,1)} %get-tuple-element.5) | data formatting | bytes 4718592
  170.4 7.8 %copy.89 = bf16[16,144,1,8,64]{1,4,3,0,2:T(8,128)(2,1)} copy(bf16[16,144,1,8,64]{4,3,2,1,0:T(8,128)(2,1)} %get-tuple-element.6) | data formatting | bytes 4718592
  178.2 7.8 %copy.90 = bf16[16,144,1,8,64]{1,4,3,0,2:T(8,128)(2,1)} copy(bf16[16,144,1,8,64]{4,3,2,1,0:T(8,128)(2,1)} %get-tuple-element.7) | data formatting | bytes 4718592
  186.0 12.8 %fusion.57 = f32[16,8,144,144]{2,3,1,0:T(8,128)} fusion(bf16[16,144,1,8,64]{1,4,3,0,2:T(8,128)(2,1)} %copy.90, bf16[16,144,1,8,64]{1,4,3,0,2:T(8,128)(2,1)} %copy.89), kind=kOutput, calls=%fused_computation.86 | convolution fusion | flops 339738624 | bytes 15335424 | tf_op jit(solution)/shard_map/nahd,nbhd->nhab/dot_general | solution.py:83
  198.7 20.3 %fusion.120 = (f32[16,8,144]{2,1,0:T(8,128)S(1)}, f32[16,8,144,144]{2,3,1,0:T(8,128)}) fusion(f32[16,8,144,144]{2,3,1,0:T(8,128)} %fusion.57, f32[8,144,144]{1,2,0:T(8,128)S(1)} %bitcast.61, pred[16,144,144]{1,2,0:T(8,128)(4,1)S(1)} %copy-done.6), kind=kOutput, calls=%fused_computation.163 | output fusion | flops 21233808 | bytes 22302720 | tf_op jit(solution)/shard_map/sub | solution.py:92
  219.1 11.3 %convert_bitcast_fusion = bf16[16,144,8,64]{1,3,2,0:T(8,128)(2,1)} fusion(f32[16,8,144,144]{2,3,1,0:T(8,128)} %get-tuple-element.9, f32[16,8,144]{2,1,0:T(8,128)S(1)} %get-tuple-element.8, bf16[16,144,1,8,64]{1,4,3,0,2:T(8,128)(2,1)} %copy.88), kind=kOutput, calls=%fused_computation.90 | convolution fusion | flops 346226688 | bytes 15409152 | tf_op jit(solution)/shard_map/nhab,nbhd->nahd/dot_general | solution.py:94
  230.3 6.7 %copy.80 = bf16[16,144,8,64]{1,0,3,2:T(8,128)(2,1)} copy(bf16[16,144,8,64]{1,3,2,0:T(8,128)(2,1)} %convert_bitcast_fusion) | data formatting | bytes 4718592 | tf_op jit(solution)/shard_map/convert_element_type | solution.py:96
  237.1 8.0 %reshape.175 = bf16[2304,512]{0,1:T(8,128)(2,1)} reshape(bf16[16,144,8,64]{1,0,3,2:T(8,128)(2,1)} %copy.80) | data formatting | bytes 4718592 | tf_op jit(solution)/shard_map/reshape | solution.py:97
  250.8 46.4 %fusion.3.clone.8 = bf16[2304,2048]{1,0:T(8,128)(2,1)S(1)} fusion(bf16[512,2048]{1,0:T(8,128)(2,1)S(1)} %copy-done, f32[2048]{0:T(1024)S(1)} %copy-done.14, f32[2304,512]{1,0:T(8,128)S(1)} %get-tuple-element.11, f32[512]{0:T(512)S(1)} %copy-done.19, f32[512]{0:T(512)S(1)} %copy-done.20, ...), kind=kOutput, calls=%fused_computation.5.clone.clone.clone.clone.clone.clone.clone.1 | convolution fusion | flops 5149163520 | bytes 16283648 | tf_op jit(solution)/shard_map/dot_general | solution.py:103
  297.2 7.0 %fusion.50 = f32[2304,512]{1,0:T(8,128)} fusion(f32[2304,512]{1,0:T(8,128)S(1)} %get-tuple-element.11, bf16[2048,512]{1,0:T(8,128)(2,1)S(1)} %copy-done.12, f32[512]{0:T(512)S(1)} %copy-done.21, bf16[2304,2048]{1,0:T(8,128)(2,1)S(1)} %fusion.3.clone.8), kind=kOutput, calls=%fused_computation.65 | convolution fusion | flops 4834197504 | bytes 20973568 | tf_op jit(solution)/shard_map/dot_general | solution.py:106
  310.7 9.2 %copy.81 = f32[2,2,4,6,2,12,512]{6,1,0,5,4,3,2:T(2,128)} copy(f32[2,2,4,6,2,12,512]{6,5,3,1,0,4,2:T(8,128)} %bitcast.58) | data formatting | bytes 9437184 | tf_op jit(solution)/shard_map/transpose | solution.py:53
  319.9 7.8 %reshape.176 = f32[4,24,24,512]{3,0,2,1:T(4,128)} reshape(f32[2,2,4,6,2,12,512]{6,1,0,5,4,3,2:T(2,128)} %copy.81) | data formatting | bytes 9437184 | tf_op jit(solution)/shard_map/reshape | solution.py:53
  332.3 17.9 %collective-permute-done.7 = f32[4,3,24,512]{3,0,2,1:T(4,128)S(1)} collective-permute-done((f32[4,3,24,512]{3,0,2,1:T(4,128)S(1)}, f32[4,3,24,512]{3,0,2,1:T(4,128)S(1)}, u32[]{:S(2)}, u32[]{:S(2)}) %collective-permute-start.7) | collective-permute-done | bytes 589856 | tf_op jit(solution)/shard_map/ppermute | solution.py:17
  350.3 10.3 %collective-permute-start.8 = (f32[4,3,6,512]{3,0,2,1:T(4,128)S(1)}, f32[4,3,6,512]{3,0,2,1:T(4,128)S(1)}, u32[]{:S(2)}, u32[]{:S(2)}) collective-permute-start(f32[4,3,6,512]{3,0,2,1:T(4,128)S(1)} %slice.111), channel_id=1, source_target_pairs={{0,15},{1,0},{2,1},{3,2},{4,3},{5,4},{6,5},{7,6},{8,7},{9,8},{10,9... | collective-permute-start | bytes 442376 | tf_op jit(solution)/shard_map/ppermute | solution.py:17
  375.2 10.1 %multiply_reduce_fusion = f32[4,12,12]{2,1,0:T(8,128)S(1)} fusion(f32[4,12,12]{2,1,0:T(8,128)S(1)} %broadcast_multiply_fusion.1, f32[4,12,2,12,2,512]{5,0,4,3,2,1:T(4,128)} %bitcast.55), kind=kLoop, calls=%fused_computation.81 | loop fusion | flops 3538368 | bytes 4723200 | tf_op jit(solution)/shard_map/reduce_sum | solution.py:23
  391.1 7.6 %reshape.178 = f32[576,2048]{1,0:T(8,128)} reshape(f32[4,12,12,2,2,512]{5,4,3,2,1,0:T(2,128)} %bitcast.59) | data formatting | bytes 9437184 | tf_op jit(solution)/shard_map/reshape | solution.py:113
  (122 shorter events, 100.0 us)
Async XLA Ops:
  0.0 250.7 %copy-start = (bf16[512,2048]{1,0:T(8,128)(2,1)S(1)}, bf16[512,2048]{1,0:T(8,128)(2,1)}, u32[]{:S(2)}) copy-start(bf16[512,2048]{1,0:T(8,128)(2,1)} %param.31) | copy-start | bytes 6291460
  0.0 13.5 %copy-start.9 = (s32[144,144]{1,0:T(8,128)S(1)}, s32[144,144]{1,0:T(8,128)}, u32[]{:S(2)}) copy-start(s32[144,144]{1,0:T(8,128)} %param.21) | copy-start | bytes 248836
  0.9 69.3 %collective-permute-start.5 = (s32[4,3,18]{2,1,0:T(4,128)S(1)}, s32[4,3,18]{2,1,0:T(4,128)S(1)}, u32[]{:S(2)}, u32[]{:S(2)}) collective-permute-start(s32[4,3,18]{2,1,0:T(4,128)S(1)} %slice.82), channel_id=1, source_target_pairs={{0,16},{16,32},{32,48},{48,64},{64,80},{80,96},{96,112},{112,0},{1... | collective-permute-start | bytes 2600 | tf_op jit(solution)/shard_map/ppermute | solution.py:17
  3.3 15.4 %collective-permute-start.3 = (s32[4,24,6]{2,1,0:T(8,128)S(1)}, s32[4,24,6]{2,1,0:T(8,128)S(1)}, u32[]{:S(2)}, u32[]{:S(2)}) collective-permute-start(s32[4,24,6]{2,1,0:T(8,128)S(1)} %slice.80), channel_id=1, source_target_pairs={{0,1},{1,2},{2,3},{3,4},{4,5},{5,6},{6,7},{7,8},{8,9},{9,10},{10,1... | collective-permute-start | bytes 6920 | tf_op jit(solution)/shard_map/ppermute | solution.py:17
  8.6 69.5 %collective-permute-start.2 = (f32[4,3,18,512]{3,2,1,0:T(8,128)}, f32[4,3,18,512]{3,2,1,0:T(8,128)S(1)}, u32[]{:S(2)}, u32[]{:S(2)}) collective-permute-start(f32[4,3,18,512]{3,2,1,0:T(8,128)} %slice.74), channel_id=1, source_target_pairs={{0,16},{16,32},{32,48},{48,64},{64,80},{80,96},{96,112},{112,0},{1... | collective-permute-start | bytes 1327112 | tf_op jit(solution)/shard_map/ppermute | solution.py:17
  12.6 6.8 %copy-start.10 = (f32[8,759]{1,0:T(8,128)S(1)}, f32[8,759]{1,0:T(8,128)}, u32[]{:S(2)}) copy-start(f32[8,759]{1,0:T(8,128)} %param.22) | copy-start | bytes 72868
  12.6 58.1 %collective-permute-start = (f32[4,24,6,512]{3,1,2,0:T(8,128)}, f32[4,24,6,512]{3,1,2,0:T(8,128)}, u32[]{:S(2)}, u32[]{:S(2)}) collective-permute-start(f32[4,24,6,512]{3,1,2,0:T(8,128)} %copy.87), channel_id=1, source_target_pairs={{0,1},{1,2},{2,3},{3,4},{4,5},{5,6},{6,7},{7,8},{8,9},{9,10},{10,1... | collective-permute-start | bytes 3538952 | tf_op jit(solution)/shard_map/ppermute | solution.py:17
  18.6 51.6 %collective-permute-start.4 = (s32[4,3,6]{2,1,0:T(4,128)S(1)}, s32[4,3,6]{2,1,0:T(4,128)S(1)}, u32[]{:S(2)}, u32[]{:S(2)}) collective-permute-start(s32[4,3,6]{2,1,0:T(4,128)S(1)} %slice.102), channel_id=1, source_target_pairs={{0,16},{16,32},{32,48},{48,64},{64,80},{80,96},{96,112},{112,0},{1... | collective-permute-start | bytes 872 | tf_op jit(solution)/shard_map/ppermute | solution.py:17
  58.5 11.7 %copy-start.8 = (s32[4,24,24]{2,1,0:T(8,128)S(1)}, s32[4,24,24]{2,1,0:T(8,128)}, u32[]{:S(2)}) copy-start(s32[4,24,24]{2,1,0:T(8,128)} %param.20) | copy-start | bytes 27652
  71.7 6.3 %collective-permute-start.1 = (f32[4,3,6,512]{3,1,2,0:T(4,128)S(1)}, f32[4,3,6,512]{3,1,2,0:T(4,128)S(1)}, u32[]{:S(2)}, u32[]{:S(2)}) collective-permute-start(f32[4,3,6,512]{3,1,2,0:T(4,128)S(1)} %slice.98), channel_id=1, source_target_pairs={{0,16},{16,32},{32,48},{48,64},{64,80},{80,96},{96,112},{112,0},{1... | collective-permute-start | bytes 442376 | tf_op jit(solution)/shard_map/ppermute | solution.py:17
  116.2 6.8 %copy-start.18 = (f32[512]{0:T(512)S(1)}, f32[512]{0:T(512)}, u32[]{:S(2)}) copy-start(f32[512]{0:T(512)} %param.23) | copy-start | bytes 6148
  186.0 12.8 %copy-start.5 = (f32[144,144,8]{0,1,2:T(8,128)S(1)}, f32[144,144,8]{0,1,2:T(8,128)}, u32[]{:S(2)}) copy-start(f32[144,144,8]{0,1,2:T(8,128)} %copy.78) | copy-start | bytes 1990660
  186.0 12.8 %copy-start.6 = (pred[16,144,144]{1,2,0:T(8,128)(4,1)S(1)}, pred[16,144,144]{1,2,0:T(8,128)(4,1)}, u32[]{:S(2)}) copy-start(pred[16,144,144]{1,2,0:T(8,128)(4,1)} %compare_and_fusion) | copy-start | bytes 995332
  237.1 8.0 %copy-start.7 = (bf16[512,512]{1,0:T(8,128)(2,1)S(1)}, bf16[512,512]{1,0:T(8,128)(2,1)}, u32[]{:S(2)}) copy-start(bf16[512,512]{1,0:T(8,128)(2,1)} %param.27) | copy-start | bytes 1572868
  237.1 8.0 %copy-start.11 = (f32[512]{0:T(512)S(1)}, f32[512]{0:T(512)}, u32[]{:S(2)}) copy-start(f32[512]{0:T(512)} %param.28) | copy-start | bytes 6148
  250.8 46.4 %copy-start.12 = (bf16[2048,512]{1,0:T(8,128)(2,1)S(1)}, bf16[2048,512]{1,0:T(8,128)(2,1)}, u32[]{:S(2)}) copy-start(bf16[2048,512]{1,0:T(8,128)(2,1)} %param.33) | copy-start | bytes 6291460
  250.8 46.4 %copy-start.21 = (f32[512]{0:T(512)S(1)}, f32[512]{0:T(512)}, u32[]{:S(2)}) copy-start(f32[512]{0:T(512)} %param.34) | copy-start | bytes 6148
  329.0 36.4 %collective-permute-start.6 = (f32[4,21,6,512]{3,0,2,1:T(4,128)S(1)}, f32[4,21,6,512]{3,0,2,1:T(4,128)S(1)}, u32[]{:S(2)}, u32[]{:S(2)}) collective-permute-start(f32[4,21,6,512]{3,0,2,1:T(4,128)S(1)} %slice.108), channel_id=1, source_target_pairs={{0,15},{1,0},{2,1},{3,2},{4,3},{5,4},{6,5},{7,6},{8,7},{9,8},{10,9... | collective-permute-start | bytes 3096584 | tf_op jit(solution)/shard_map/ppermute | solution.py:17
  331.5 18.8 %collective-permute-start.7 = (f32[4,3,24,512]{3,0,2,1:T(4,128)S(1)}, f32[4,3,24,512]{3,0,2,1:T(4,128)S(1)}, u32[]{:S(2)}, u32[]{:S(2)}) collective-permute-start(f32[4,3,24,512]{3,0,2,1:T(4,128)S(1)} %slice.109), channel_id=1, source_target_pairs={{0,112},{16,0},{32,16},{48,32},{64,48},{80,64},{96,80},{112,96},{1... | collective-permute-start | bytes 1769480 | tf_op jit(solution)/shard_map/ppermute | solution.py:17
  350.3 15.1 %collective-permute-start.8 = (f32[4,3,6,512]{3,0,2,1:T(4,128)S(1)}, f32[4,3,6,512]{3,0,2,1:T(4,128)S(1)}, u32[]{:S(2)}, u32[]{:S(2)}) collective-permute-start(f32[4,3,6,512]{3,0,2,1:T(4,128)S(1)} %slice.111), channel_id=1, source_target_pairs={{0,15},{1,0},{2,1},{3,2},{4,3},{5,4},{6,5},{7,6},{8,7},{9,8},{10,9... | collective-permute-start | bytes 442376 | tf_op jit(solution)/shard_map/ppermute | solution.py:17
  375.2 10.1 %copy-start.3 = (f32[4,24,24,512]{3,0,2,1:T(4,128)S(1)}, f32[4,24,24,512]{3,0,2,1:T(4,128)}, u32[]{:S(2)}) copy-start(f32[4,24,24,512]{3,0,2,1:T(4,128)} %copy-done.2) | copy-start | bytes 14155780
  391.1 7.7 %copy-start.15 = (f32[2048]{0:T(1024)S(1)}, f32[2048]{0:T(1024)}, u32[]{:S(2)}) copy-start(f32[2048]{0:T(1024)} %param.36) | copy-start | bytes 24580
  391.1 7.7 %copy-start.16 = (f32[2048]{0:T(1024)S(1)}, f32[2048]{0:T(1024)}, u32[]{:S(2)}) copy-start(f32[2048]{0:T(1024)} %param.35) | copy-start | bytes 24580
  398.8 11.1 %copy-start.1 = (bf16[512,2048]{1,0:T(8,128)(2,1)S(1)}, bf16[512,2048]{1,0:T(8,128)(2,1)}, u32[]{:S(2)}) copy-start(bf16[512,2048]{1,0:T(8,128)(2,1)} %param.31) | copy-start | bytes 6291460
  (7 other events, 20.9 us)
where the time goes:
time: 418 us; the launch traced here: 410 us
  local copies, waits for them, and re-layouts  215 us (51%)
  matrix products  97 us (23%)
  other arithmetic  55.2 us (13%)
  waiting for transfers between devices  21.4 us (5%)
  starting transfers between devices  21.1 us (5%)
    gather x2, local copies, waits for them, and re-layouts, per_device(): pair_bias = rel_table[:, rel_index]  50.6 us
    dot_general x1, matrix products, window_block(): jnp.dot(normed2, fc1_weight, preferred_element_type=jnp.float32) + fc1_bias  46.4 us
    unnamed x49, local copies, waits for them, and re-layouts  29.2 us
    ppermute x9, waiting for transfers between devices, shifted(): return lax.ppermute(value, axis, pairs)  21.4 us
    ppermute x9, starting transfers between devices, shifted(): return lax.ppermute(value, axis, pairs)  21.1 us
    sub x1, other arithmetic, window_block(): powers = jnp.exp(scores - row_max)  20.3 us
    reshape x1, local copies, waits for them, and re-layouts, window_block(): packed = packed.reshape(win_count, win_tokens, 3, num_heads, head_size)  18 us
    reduce_sum x3, other arithmetic, layer_norm(): variance = jnp.mean(centred * centred, -1, keepdims=True)  17.1 us
  transfers between devices with their start and end apart: 9, of which 3 were waited for; matrix products, arithmetic and copies ran while one was open for 17% of the time, Pallas kernels for 0%

commit v1 on v0

v1 whole, which is shorter than its diff:
```python
import functools

import jax
import jax.numpy as jnp
from jax import lax
from jax.experimental import pallas as pl
from jax.experimental.pallas import tpu as pltpu
from jax.sharding import PartitionSpec as P

MESH = pl.DeviceIdType.MESH
F32 = jnp.float32
BF16 = jnp.bfloat16
EPS = 1e-05
SIDE = 24
WTOK = 144
G = 4
ROWS = G * WTOK
TOKENS = 4 * SIDE * SIDE
TILES = 4
SLOT = 72

LEVELS = ((1, 2), (3, 0))
CORNER = ((-3, -6), (3, 6))
PIECES = (
    ((3, 6, 18, 6), (9, 6, 18, 6), (15, 6, 18, 6), (0, 3, 18, 6), (21, 3, 6, 12), (21, 3, 0, 6), (21, 3, 18, 6)),
    ((3, 6, 0, 6), (9, 6, 0, 6), (15, 6, 0, 6), (21, 3, 0, 6), (0, 3, 6, 12), (0, 3, 18, 6), (0, 3, 0, 6)),
)
FROM = ((0, -1), (0, -1), (0, -1), (0, -1), (-1, 0), (-1, 0), (-1, -1))
STEPS = (
    ((0, 1, 1), (0, 2, 1), (1, 0, 0), (1, 1, 0)),
    ((0, 1, 0), (0, 2, 0), (1, 0, 1), (1, 1, 1)),
    ((0, 0, 0), (0, 0, 1), (1, 3, 1), (1, 3, 0)),
    ((0, 3, 0), (1, 2, 1), (0, 3, 1), (1, 2, 0)),
)


def segments(window):
    pair, wrow, wcol = window
    row0, col0 = CORNER[pair][0] + 6 * wrow, CORNER[pair][1] + 12 * wcol
    runs = []
    for lev in range(2):
        for row in range(6):
            for half in range(2):
                at_row, at_col = row0 + row, col0 + 6 * half
                where_row, where_col = at_row % SIDE, at_col % SIDE
                away = (at_row // SIDE, at_col // SIDE)
                token = (lev * 6 + row) * 12 + 6 * half
                if away == (0, 0):
                    slot, first = None, (LEVELS[pair][lev] * SIDE + where_row) * SIDE + where_col
                else:
                    slot = None
                    for number, (first_row, rows, first_col, cols) in enumerate(PIECES[pair]):
                        if first_row <= where_row < first_row + rows and first_col <= where_col < first_col + cols:
                            slot = number
                            first = (lev * rows + where_row - first_row) * cols + where_col - first_col
                if runs and runs[-1][2] == slot and runs[-1][0] + runs[-1][1] == token and runs[-1][3] + runs[-1][1] == first:
                    runs[-1] = (runs[-1][0], runs[-1][1] + 6, slot, runs[-1][3])
                else:
                    runs.append((token, 6, slot, first))
    return runs


def slots_of(windows):
    return [
        (window[0], slot)
        for window in windows
        for slot in sorted({run[2] for run in segments(window) if run[2] is not None})
    ]


def piece_runs(pair, slot):
    first_row, rows, first_col, cols = PIECES[pair][slot]
    for lev in range(2):
        for row in range(rows):
            yield (lev * rows + row) * cols, cols, (LEVELS[pair][lev] * SIDE + first_row + row) * SIDE + first_col


def norm(values, gain, shift):
    centred = values - jnp.mean(values, -1, keepdims=True)
    variance = jnp.mean(centred * centred, -1, keepdims=True)
    return centred * lax.rsqrt(variance + EPS) * gain + shift


def wide(ref, first, count):
    return jnp.concatenate([ref[tile, pl.ds(first, count), :] for tile in range(TILES)], 1)


def put_wide(ref, first, count, values):
    for tile in range(TILES):
        ref[tile, pl.ds(first, count), :] = values[:, 128 * tile : 128 * (tile + 1)]


def make_bias(rel_index, rel_table, bias):
    def rows_at(step, _):
        at = pl.multiple_of(step * 8, 8)
        for first, count in ((0, 128), (128, 16)):
            index = rel_index[pl.ds(at, 8), pl.ds(first, count)]
            if count < 128:
                index = jnp.concatenate([index, jnp.zeros((8, 128 - count), jnp.int32)], 1)
            low, high = index & 127, index >> 7
            for head in range(8):
                found = jnp.zeros((8, 128), F32)
                for part in range(6):
                    row = rel_table[pl.ds(head, 1), pl.ds(128 * part, 128)]
                    drawn = jnp.take_along_axis(
                        jnp.broadcast_to(row, (8, 128)), low, axis=1, mode="promise_in_bounds"
                    )
                    found = jnp.where(high == part, drawn, found)
                bias[head, pl.ds(at, 8), pl.ds(first, count)] = found[:, :count]
        return 0

    lax.fori_loop(0, WTOK // 8, rows_at, 0)


def attend(qkv, attended, bias, marks, first):
    lane = lax.broadcasted_iota(jnp.int32, (1, 128), 1)
    left = lane < 64
    mark = marks[pl.ds(first, WTOK), :]
    barred = jnp.where(mark > 0, jnp.zeros_like(mark), jnp.full_like(mark, -1e30))
    ones = jnp.ones((WTOK, 128), BF16)
    for pair in range(4):
        query = qkv[pl.ds(first, WTOK), pl.ds(128 * pair, 128)]
        key = qkv[pl.ds(first, WTOK), pl.ds(512 + 128 * pair, 128)]
        value = qkv[pl.ds(first, WTOK), pl.ds(1024 + 128 * pair, 128)]
        keys = jnp.concatenate([key, barred], 1)
        values = jnp.concatenate([value, ones], 1)
        zero = jnp.zeros_like(query)
        results = []
        for side in range(2):
            part = jnp.where(left, query, zero) if side == 0 else jnp.where(left, zero, query)
            scores = lax.dot_general(
                jnp.concatenate([part, mark], 1), keys, (((1,), (1,)), ((), ())), preferred_element_type=F32
            )
            scores = scores + bias[2 * pair + side]
            powers = jnp.exp(scores - jnp.max(scores, -1, keepdims=True)).astype(BF16)
            total = jnp.dot(powers, values, preferred_element_type=F32)
            results.append(total[:, :128] / total[:, 128:])
        attended[pl.ds(first, WTOK), pl.ds(128 * pair, 128)] = jnp.where(left, results[0], results[1]).astype(BF16)


def mark_window(ids, marks, window, first, lat, lat_count):
    pair, wrow, wcol = window
    row0, col0 = CORNER[pair][0] + 6 * wrow, CORNER[pair][1] + 12 * wcol
    token = lax.broadcasted_iota(jnp.int32, (WTOK, 1), 0)
    lev, row, col = token // 72, token // 12 % 6, token % 12
    at_row = row0 + row
    line = lev * SIDE + (at_row + SIDE) % SIDE
    pick = lax.broadcasted_iota(jnp.int32, (WTOK, 2 * SIDE), 1) == line
    rows = jnp.dot(jnp.where(pick, 1.0, 0.0).astype(BF16), ids[pair].astype(BF16), preferred_element_type=F32)
    lane = lax.broadcasted_iota(jnp.int32, (WTOK, 128), 1)
    region = jnp.sum(jnp.where(lane == (col0 + col + SIDE) % SIDE, rows, 0.0), -1, keepdims=True)
    whole = lat_count * SIDE
    orig = lat * SIDE + at_row
    orig = jnp.where(orig < 0, orig + whole, jnp.where(orig >= whole, orig - whole, orig))
    band = jnp.where(orig >= whole - 3, 1, 0)
    if pair == 1:
        band = band + 2 * lev
    kind = region.astype(jnp.int32) + 3 * band
    marks[pl.ds(first, WTOK), :] = jnp.where(lane == kind, 1.0, 0.0).astype(BF16)


def kernel(
    lat_count,
    lon_count,
    tokens,
    qkv_weight,
    proj_weight,
    fc1_weight,
    fc2_weight,
    merge_weight,
    region,
    rel_index,
    rel_table,
    norm1_gain,
    norm1_bias,
    qkv_bias,
    proj_bias,
    norm2_gain,
    norm2_bias,
    fc1_bias,
    fc2_bias,
    merge_gain,
    merge_bias,
    out,
    block,
    part,
    wq,
    wp,
    w1,
    w2,
    wm,
    bias,
    marks,
    normed,
    qkv,
    attended,
    active,
    normed3,
    own_ids,
    far_ids,
    ids,
    halo_out,
    halo_in,
    back_out,
    back_in,
    load_sem,
    id_send,
    id_recv,
    halo_send,
    halo_recv,
    back_send,
    back_recv,
):
    lat, lon = lax.axis_index("lat"), lax.axis_index("lon")

    def device(rows, cols):
        return lax.rem(lat + rows + lat_count, lat_count), lax.rem(lon + cols + lon_count, lon_count)

    barrier = pltpu.get_barrier_semaphore()
    around = ((0, 1), (1, 0), (1, 1), (0, -1), (-1, 0), (-1, -1))
    for away in around:
        pl.semaphore_signal(barrier, inc=1, device_id=device(*away), device_id_type=MESH)

    loads = [
        pltpu.make_async_copy(
            tokens.at[:, pl.ds(128 * tile, 128)], block.at[tile, pl.ds(0, TOKENS)], load_sem.at[tile]
        )
        for tile in range(TILES)
    ]
    for number, (source, target) in enumerate(
        ((qkv_weight, wq), (proj_weight, wp), (fc1_weight, w1), (fc2_weight, w2), (merge_weight, wm))
    ):
        loads.append(pltpu.make_async_copy(source, target, load_sem.at[TILES + number]))
    for load in loads:
        load.start()

    own_ids[...] = jnp.zeros_like(own_ids)
    for pair in range(2):
        for lev in range(2):
            own_ids[pair, pl.ds(SIDE * lev, SIDE), pl.ds(0, SIDE)] = region[LEVELS[pair][lev]].astype(F32)
    block[:, pl.ds(TOKENS, 16), :] = jnp.zeros((TILES, 16, 128), F32)
    for pair in range(2):
        for slot in (3, 5, 6):
            halo_out[pair, slot, :, pl.ds(32, 8), :] = jnp.zeros((TILES, 8, 128), F32)
            back_out[pair, slot, :, pl.ds(32, 8), :] = jnp.zeros((TILES, 8, 128), F32)

    def id_copy(pair, side):
        rows, cols = ((0, 1), (1, 0), (1, 1))[side]
        sign = 1 if pair == 0 else -1
        return pltpu.make_async_remote_copy(
            src_ref=own_ids.at[pair],
            dst_ref=far_ids.at[pair, side],
            send_sem=id_send.at[pair, side],
            recv_sem=id_recv.at[pair, side],
            device_id=device(sign * rows, sign * cols),
            device_id_type=MESH,
        )

    def piece_copy(pair, slot, back):
        rows, cols = FROM[slot]
        sign = (1 if pair == 0 else -1) * (1 if back else -1)
        size = SLOT if slot in (0, 1, 2, 4) else 40
        source, target = (back_out, back_in) if back else (halo_out, halo_in)
        send, recv = (back_send, back_recv) if back else (halo_send, halo_recv)
        return pltpu.make_async_remote_copy(
            src_ref=source.at[pair, slot, :, pl.ds(0, size)],
            dst_ref=target.at[pair, slot, :, pl.ds(0, size)],
            send_sem=send.at[pair, slot],
            recv_sem=recv.at[pair, slot],
            device_id=device(sign * rows, sign * cols),
            device_id_type=MESH,
        )

    order = [slot for step in STEPS for slot in slots_of(step)]

    pl.semaphore_wait(barrier, len(around))
    for pair in range(2):
        for side in range(3):
            id_copy(pair, side).start()
    for load in loads[:TILES]:
        load.wait()
    for pair, slot in order:
        for first, count, where in piece_runs(pair, slot):
            halo_out[pair, slot, :, pl.ds(first, count), :] = block[:, pl.ds(where, count), :]
        piece_copy(pair, slot, False).start()

    make_bias(rel_index, rel_table, bias)

    for pair in range(2):
        for side in range(3):
            id_copy(pair, side).wait()
        line = lax.broadcasted_iota(jnp.int32, (2 * SIDE, 128), 0) % SIDE
        lane = lax.broadcasted_iota(jnp.int32, (2 * SIDE, 128), 1)
        far_row = line >= SIDE - 3 if pair == 0 else line < 3
        far_col = lane >= SIDE - 6 if pair == 0 else lane < 6
        ids[pair] = jnp.where(
            far_row,
            jnp.where(far_col, far_ids[pair, 2], far_ids[pair, 1]),
            jnp.where(far_col, far_ids[pair, 0], own_ids[pair]),
        )
    for load in loads[TILES:-1]:
        load.wait()

    def run(step, _):
        for number, windows in enumerate(STEPS):

            @pl.when(step == number)
            def _():
                for pair, slot in slots_of(windows):
                    piece_copy(pair, slot, False).wait_recv()
                for place, window in enumerate(windows):
                    for token, count, slot, first in segments(window):
                        at = pl.ds(place * WTOK + token, count)
                        if slot is None:
                            part[:, at, :] = block[:, pl.ds(first, count), :]
                        else:
                            part[:, at, :] = halo_in[window[0], slot, :, pl.ds(first, count), :]
                    mark_window(ids, marks, window, place * WTOK, lat, lat_count)

        for place in range(G):
            normed[pl.ds(place * WTOK, WTOK), :] = norm(
                wide(part, place * WTOK, WTOK), norm1_gain[...], norm1_bias[...]
            ).astype(BF16)
        for third in range(3):
            columns = pl.ds(512 * third, 512)
            packed = jnp.dot(normed[...], wq[:, columns], preferred_element_type=F32) + qkv_bias[:, columns]
            if third == 0:
                packed = packed * 0.125
            qkv[:, columns] = packed.astype(BF16)
        for place in range(G):
            attend(qkv, attended, bias, marks, place * WTOK)
        hidden = jnp.dot(attended[...], wp[...], preferred_element_type=F32) + proj_bias[...] + wide(part, 0, ROWS)
        put_wide(part, 0, ROWS, hidden)
        normed[...] = norm(hidden, norm2_gain[...], norm2_bias[...]).astype(BF16)
        for quarter in range(4):
            columns = pl.ds(512 * quarter, 512)
            units = jnp.dot(normed[...], w1[:, columns], preferred_element_type=F32) + fc1_bias[:, columns]
            active[:, columns] = (0.5 * units * (1.0 + lax.erf(units * 0.7071067811865476))).astype(BF16)
        result = jnp.dot(active[...], w2[...], preferred_element_type=F32) + fc2_bias[...] + wide(part, 0, ROWS)
        put_wide(part, 0, ROWS, result)

        for number, windows in enumerate(STEPS):

            @pl.when(step == number)
            def _():
                for place, window in enumerate(windows):
                    for token, count, slot, first in segments(window):
                        at = pl.ds(place * WTOK + token, count)
                        if slot is None:
                            block[:, pl.ds(first, count), :] = part[:, at, :]
                        else:
                            back_out[window[0], slot, :, pl.ds(first, count), :] = part[:, at, :]
                for pair, slot in slots_of(windows):
                    piece_copy(pair, slot, True).start()

        return 0

    lax.fori_loop(0, len(STEPS), run, 0)

    for pair, slot in order:
        piece_copy(pair, slot, True).wait_recv()
        for first, count, where in piece_runs(pair, slot):
            block[:, pl.ds(where, count), :] = back_in[pair, slot, :, pl.ds(first, count), :]
    loads[-1].wait()

    def merge_norm(step, _):
        for number in range(4):
            line = step * 4 + number
            values = jnp.concatenate(
                [
                    block[tile, pl.ds(line * 2 * SIDE + row * SIDE + col, 16, stride=2), :]
                    for col in range(2)
                    for row in range(2)
                    for tile in range(TILES)
                ],
                1,
            )
            normed3[pl.ds(pl.multiple_of(line * 16, 16), 16), :] = norm(
                values, merge_gain[...], merge_bias[...]
            ).astype(BF16)
        return 0

    lax.fori_loop(0, 12, merge_norm, 0)
    for quarter in range(4):
        columns = pl.ds(256 * quarter, 256)
        merged = jnp.dot(normed3[...], wm[:, columns], preferred_element_type=F32).astype(BF16)
        out[:, :, columns] = merged.reshape(48, 16, 256)[:, :12]

    for pair, slot in order:
        piece_copy(pair, slot, False).wait_send()
        piece_copy(pair, slot, True).wait_send()


def per_device(mesh_shape, tokens, region, rel_index, rel_table, *rest):
    (
        norm1_gain,
        norm1_bias,
        qkv_weight,
        qkv_bias,
        proj_weight,
        proj_bias,
        norm2_gain,
        norm2_bias,
        fc1_weight,
        fc1_bias,
        fc2_weight,
        fc2_bias,
        merge_gain,
        merge_bias,
        merge_weight,
    ) = rest
    lines = [
        value.reshape(1, -1)
        for value in (
            norm1_gain,
            norm1_bias,
            qkv_bias,
            proj_bias,
            norm2_gain,
            norm2_bias,
            fc1_bias,
            fc2_bias,
            merge_gain,
            merge_bias,
        )
    ]
    rel_table = jnp.pad(rel_table, ((0, 0), (0, 768 - rel_table.shape[1])))
    hbm = pl.BlockSpec(memory_space=pl.ANY)
    vmem = pl.BlockSpec(memory_space=pltpu.VMEM)
    merged = pl.pallas_call(
        functools.partial(kernel, *mesh_shape),
        out_shape=jax.ShapeDtypeStruct((48, 12, 1024), BF16),
        in_specs=[hbm] * 6 + [vmem] * 13,
        out_specs=vmem,
        scratch_shapes=[
            pltpu.VMEM((TILES, TOKENS + 16, 128), F32),
            pltpu.VMEM((TILES, ROWS, 128), F32),
            pltpu.VMEM((512, 1536), BF16),
            pltpu.VMEM((512, 512), BF16),
            pltpu.VMEM((512, 2048), BF16),
            pltpu.VMEM((2048, 512), BF16),
            pltpu.VMEM((2048, 1024), BF16),
            pltpu.VMEM((8, WTOK, WTOK), F32),
            pltpu.VMEM((ROWS, 128), BF16),
            pltpu.VMEM((ROWS, 512), BF16),
            pltpu.VMEM((ROWS, 1536), BF16),
            pltpu.VMEM((ROWS, 512), BF16),
            pltpu.VMEM((ROWS, 2048), BF16),
            pltpu.VMEM((768, 2048), BF16),
            pltpu.VMEM((2, 2 * SIDE, 128), F32),
            pltpu.VMEM((2, 3, 2 * SIDE, 128), F32),
            pltpu.VMEM((2, 2 * SIDE, 128), F32),
        ]
        + [pltpu.VMEM((2, 7, TILES, SLOT, 128), F32)] * 4
        + [
            pltpu.SemaphoreType.DMA((TILES + 5,)),
            pltpu.SemaphoreType.DMA((2, 3)),
            pltpu.SemaphoreType.DMA((2, 3)),
        ]
        + [pltpu.SemaphoreType.DMA((2, 7))] * 4,
        compiler_params=pltpu.CompilerParams(
            collective_id=0, has_side_effects=True, vmem_limit_bytes=60 * 2**20
        ),
        name="block",
    )(
        tokens.reshape(TOKENS, 512),
        qkv_weight,
        proj_weight,
        fc1_weight,
        fc2_weight,
        merge_weight,
        region,
        rel_index,
        rel_table,
        *lines,
    )
    return merged.reshape(4, 12, 12, 1024)


def solution(mesh):
    shape = (mesh.shape["lat"], mesh.shape["lon"])
    return jax.shard_map(
        functools.partial(per_device, shape),
        mesh=mesh,
        in_specs=(P(None, "lat", "lon", None), P(None, "lat", "lon")) + (P(),) * 17,
        out_specs=P(None, "lat", "lon", None),
        check_vma=False,
    )
```

time: 418 us -> 63.8 us (0.15)
  the two profiles are of different devices: /device:TPU:59 before, /device:TPU:0 now
where the time goes in v1:
time: 63.8 us; the launch traced here: 63.6 us
  Pallas kernels  57.6 us (90%)
  local copies, waits for them, and re-layouts  5.99 us (9%)
    pallas_call x1, Pallas kernels, per_device(): pl.pallas_call(functools.partial(kernel, *mesh_shape), out_shape=jax.Shap...  57.6 us
    reshape x1, local copies, waits for them, and re-layouts, per_device(): return merged.reshape(4, 12, 12, 1024)  3.35 us
    pad x1, local copies, waits for them, and re-layouts, per_device(): rel_table = jnp.pad(rel_table, ((0, 0), (0, 768 - rel_table.shape[1])))  1.35 us
    reshape x1, local copies, waits for them, and re-layouts, per_device(): value.reshape(1, -1)  1.29 us

profile of v1, /device:TPU:0, one launch (start us, length us, event | category | flops | bytes accessed | tf_op | source)
XLA Modules:
  0.0 63.6 jit_solution(11529169570132092621)
XLA Ops:
  0.0 1.3 %reshape.39.qkv_bias = f32[1,1536]{1,0:T(1,128)} reshape(f32[1536]{0:T(1024)} %param.26) | data formatting | bytes 12288 | tf_op jit(solution)/shard_map/reshape | solution.py:413
  1.3 1.3 %pad.4.rel_table = f32[8,768]{1,0:T(8,128)} pad(f32[8,759]{1,0:T(8,128)} %param.22, f32[]{:T(128)} %constant.2.clone.1), padding=0_0x0_9 | pad | bytes 48868 | tf_op jit(solution)/shard_map/jit(_pad)/pad | solution.py:427
  2.6 57.6 %block.1 = bf16[48,12,1024]{2,1,0:T(8,128)(2,1)} custom-call(f32[2304,512]{1,0:T(8,128)} %bitcast.12, bf16[512,1536]{1,0:T(8,128)(2,1)} %qkv_weight.1, bf16[512,512]{1,0:T(8,128)(2,1)} %proj_weight.1, bf16[512,2048]{1,0:T(8,128)(2,1)} %fc1_weight.1, bf16[2048,512]{1,0:T(8,128)(2,1)} %fc2_weight.1, bf16[2048,1024]{1,0:T(8,128)(2,1)} %merge_weight.1, ...), custom_call_target="tpu_custom_call" | custom-call | tf_op jit(solution)/shard_map/block/pallas_call | solution.py:430
  60.2 3.3 %copy.20 = bf16[4,12,12,1024]{3,0,2,1:T(4,128)(2,1)} copy(bf16[4,12,12,1024]{3,2,1,0:T(8,128)(2,1)} %bitcast.11) | data formatting | bytes 2359296 | tf_op jit(solution)/shard_map/reshape | solution.py:477

commit v2 on v1

--- a/solution.py
+++ b/solution.py
@@ -28,9 +28,9 @@
 FROM = ((0, -1), (0, -1), (0, -1), (0, -1), (-1, 0), (-1, 0), (-1, -1))
 STEPS = (
     ((0, 1, 1), (0, 2, 1), (1, 0, 0), (1, 1, 0)),
-    ((0, 1, 0), (0, 2, 0), (1, 0, 1), (1, 1, 1)),
-    ((0, 0, 0), (0, 0, 1), (1, 3, 1), (1, 3, 0)),
-    ((0, 3, 0), (1, 2, 1), (0, 3, 1), (1, 2, 0)),
+    ((0, 1, 0), (0, 2, 0), (0, 3, 0), (0, 0, 1)),
+    ((0, 0, 0), (1, 3, 1), (1, 0, 1), (1, 1, 1)),
+    ((1, 2, 1), (1, 3, 0), (0, 3, 1), (1, 2, 0)),
 )
 
 
@@ -90,7 +90,10 @@
         ref[tile, pl.ds(first, count), :] = values[:, 128 * tile : 128 * (tile + 1)]
 
 
-def make_bias(rel_index, rel_table, bias):
+def make_bias(rel_index, rel_table, table, bias):
+    table[...] = jnp.zeros_like(table)
+    table[:, pl.ds(0, rel_table.shape[1])] = rel_table[...]
+
     def rows_at(step, _):
         at = pl.multiple_of(step * 8, 8)
         for first, count in ((0, 128), (128, 16)):
@@ -101,7 +104,7 @@
             for head in range(8):
                 found = jnp.zeros((8, 128), F32)
                 for part in range(6):
-                    row = rel_table[pl.ds(head, 1), pl.ds(128 * part, 128)]
+                    row = table[pl.ds(head, 1), pl.ds(128 * part, 128)]
                     drawn = jnp.take_along_axis(
                         jnp.broadcast_to(row, (8, 128)), low, axis=1, mode="promise_in_bounds"
                     )
@@ -196,6 +199,8 @@
     attended,
     active,
     normed3,
+    product,
+    table,
     own_ids,
     far_ids,
     ids,
@@ -221,18 +226,20 @@
     for away in around:
         pl.semaphore_signal(barrier, inc=1, device_id=device(*away), device_id_type=MESH)
 
-    loads = [
-        pltpu.make_async_copy(
+    def token_load(tile):
+        return pltpu.make_async_copy(
             tokens.at[:, pl.ds(128 * tile, 128)], block.at[tile, pl.ds(0, TOKENS)], load_sem.at[tile]
         )
-        for tile in range(TILES)
+
+    for tile in range(TILES):
+        token_load(tile).start()
+
+    loads = [
+        pltpu.make_async_copy(source, target, load_sem.at[TILES + number])
+        for number, (source, target) in enumerate(
+            ((qkv_weight, wq), (proj_weight, wp), (fc1_weight, w1), (fc2_weight, w2), (merge_weight, wm))
+        )
     ]
-    for number, (source, target) in enumerate(
-        ((qkv_weight, wq), (proj_weight, wp), (fc1_weight, w1), (fc2_weight, w2), (merge_weight, wm))
-    ):
-        loads.append(pltpu.make_async_copy(source, target, load_sem.at[TILES + number]))
-    for load in loads:
-        load.start()
 
     own_ids[...] = jnp.zeros_like(own_ids)
     for pair in range(2):
@@ -273,32 +280,38 @@
 
     order = [slot for step in STEPS for slot in slots_of(step)]
 
+    for tile in range(TILES):
+        token_load(tile).wait()
+    for load in loads:
+        load.start()
+    for pair, slot in order:
+        for first, count, where in piece_runs(pair, slot):
+            halo_out[pair, slot, :, pl.ds(first, count), :] = block[:, pl.ds(where, count), :]
     pl.semaphore_wait(barrier, len(around))
     for pair in range(2):
         for side in range(3):
             id_copy(pair, side).start()
-    for load in loads[:TILES]:
-        load.wait()
     for pair, slot in order:
-        for first, count, where in piece_runs(pair, slot):
-            halo_out[pair, slot, :, pl.ds(first, count), :] = block[:, pl.ds(where, count), :]
         piece_copy(pair, slot, False).start()
 
-    make_bias(rel_index, rel_table, bias)
-
-    for pair in range(2):
-        for side in range(3):
-            id_copy(pair, side).wait()
-        line = lax.broadcasted_iota(jnp.int32, (2 * SIDE, 128), 0) % SIDE
-        lane = lax.broadcasted_iota(jnp.int32, (2 * SIDE, 128), 1)
-        far_row = line >= SIDE - 3 if pair == 0 else line < 3
-        far_col = lane >= SIDE - 6 if pair == 0 else lane < 6
-        ids[pair] = jnp.where(
-            far_row,
-            jnp.where(far_col, far_ids[pair, 2], far_ids[pair, 1]),
-            jnp.where(far_col, far_ids[pair, 0], own_ids[pair]),
-        )
-    for load in loads[TILES:-1]:
+    ids[...] = own_ids[...]
+    make_bias(rel_index, rel_table, table, bias)
+
+    def all_ids():
+        for pair in range(2):
+            for side in range(3):
+                id_copy(pair, side).wait()
+            line = lax.broadcasted_iota(jnp.int32, (2 * SIDE, 128), 0) % SIDE
+            lane = lax.broadcasted_iota(jnp.int32, (2 * SIDE, 128), 1)
+            far_row = line >= SIDE - 3 if pair == 0 else line < 3
+            far_col = lane >= SIDE - 6 if pair == 0 else lane < 6
+            ids[pair] = jnp.where(
+                far_row,
+                jnp.where(far_col, far_ids[pair, 2], far_ids[pair, 1]),
+                jnp.where(far_col, far_ids[pair, 0], own_ids[pair]),
+            )
+
+    for load in loads[:-1]:
         load.wait()
 
     def run(step, _):
@@ -306,6 +319,8 @@
 
             @pl.when(step == number)
             def _():
+                if number == 1:
+                    all_ids()
                 for pair, slot in slots_of(windows):
                     piece_copy(pair, slot, False).wait_recv()
                 for place, window in enumerate(windows):
@@ -323,7 +338,7 @@
             ).astype(BF16)
         for third in range(3):
             columns = pl.ds(512 * third, 512)
-            packed = jnp.dot(normed[...], wq[:, columns], preferred_element_type=F32) + qkv_bias[:, columns]
+            packed = jnp.dot(normed[...], wq[:, columns], preferred_element_type=F32) + qkv_bias[columns].reshape(1, 512)
             if third == 0:
                 packed = packed * 0.125
             qkv[:, columns] = packed.astype(BF16)
@@ -357,34 +372,46 @@
 
     lax.fori_loop(0, len(STEPS), run, 0)
 
-    for pair, slot in order:
-        piece_copy(pair, slot, True).wait_recv()
-        for first, count, where in piece_runs(pair, slot):
-            block[:, pl.ds(where, count), :] = back_in[pair, slot, :, pl.ds(first, count), :]
-    loads[-1].wait()
-
-    def merge_norm(step, _):
-        for number in range(4):
-            line = step * 4 + number
-            values = jnp.concatenate(
-                [
-                    block[tile, pl.ds(line * 2 * SIDE + row * SIDE + col, 16, stride=2), :]
-                    for col in range(2)
-                    for row in range(2)
-                    for tile in range(TILES)
-                ],
-                1,
-            )
-            normed3[pl.ds(pl.multiple_of(line * 16, 16), 16), :] = norm(
-                values, merge_gain[...], merge_bias[...]
-            ).astype(BF16)
-        return 0
-
-    lax.fori_loop(0, 12, merge_norm, 0)
-    for quarter in range(4):
-        columns = pl.ds(256 * quarter, 256)
-        merged = jnp.dot(normed3[...], wm[:, columns], preferred_element_type=F32).astype(BF16)
-        out[:, :, columns] = merged.reshape(48, 16, 256)[:, :12]
+    def merge(pair):
+        for other, slot in order:
+            if other == pair:
+                piece_copy(pair, slot, True).wait_recv()
+                for first, count, where in piece_runs(pair, slot):
+                    block[:, pl.ds(where, count), :] = back_in[pair, slot, :, pl.ds(first, count), :]
+        if pair == 0:
+            loads[-1].wait()
+
+        def merge_norm(step, _):
+            for number in range(4):
+                at = step * 4 + number
+                line = at + 12 if pair == 0 else lax.rem(at + 36, 48)
+                values = jnp.concatenate(
+                    [
+                        block[tile, pl.ds(line * 2 * SIDE + row * SIDE + col, 16, stride=2), :]
+                        for col in range(2)
+                        for row in range(2)
+                        for tile in range(TILES)
+                    ],
+                    1,
+                )
+                normed3[pl.ds(pl.multiple_of(at * 16, 16), 16), :] = norm(
+                    values, merge_gain[...], merge_bias[...]
+                ).astype(BF16)
+            return 0
+
+        lax.fori_loop(0, 6, merge_norm, 0)
+        for quarter in range(4):
+            merged = jnp.dot(normed3[...], wm[:, pl.ds(256 * quarter, 256)], preferred_element_type=F32)
+            for at in range(24):
+                for half in range(2):
+                    product[
+                        2 * quarter + half, pl.ds(at % 12 * 48 + LEVELS[pair][at // 12], 12, stride=4), :
+                    ] = merged[16 * at : 16 * at + 12, 128 * half : 128 * (half + 1)]
+
+    merge(0)
+    merge(1)
+    for tile in range(8):
+        out[:, :, pl.ds(128 * tile, 128)] = product[tile].astype(BF16).reshape(144, 4, 128)
 
     for pair, slot in order:
         piece_copy(pair, slot, False).wait_send()
@@ -414,7 +441,6 @@
         for value in (
             norm1_gain,
             norm1_bias,
-            qkv_bias,
             proj_bias,
             norm2_gain,
             norm2_bias,
@@ -424,12 +450,12 @@
             merge_bias,
         )
     ]
-    rel_table = jnp.pad(rel_table, ((0, 0), (0, 768 - rel_table.shape[1])))
+    lines.insert(2, qkv_bias)
     hbm = pl.BlockSpec(memory_space=pl.ANY)
     vmem = pl.BlockSpec(memory_space=pltpu.VMEM)
     merged = pl.pallas_call(
         functools.partial(kernel, *mesh_shape),
-        out_shape=jax.ShapeDtypeStruct((48, 12, 1024), BF16),
+        out_shape=jax.ShapeDtypeStruct((144, 4, 1024), BF16),
         in_specs=[hbm] * 6 + [vmem] * 13,
         out_specs=vmem,
         scratch_shapes=[
@@ -446,7 +472,9 @@
             pltpu.VMEM((ROWS, 1536), BF16),
             pltpu.VMEM((ROWS, 512), BF16),
             pltpu.VMEM((ROWS, 2048), BF16),
-            pltpu.VMEM((768, 2048), BF16),
+            pltpu.VMEM((384, 2048), BF16),
+            pltpu.VMEM((8, 576, 128), F32),
+            pltpu.VMEM((8, 768), F32),
             pltpu.VMEM((2, 2 * SIDE, 128), F32),
             pltpu.VMEM((2, 3, 2 * SIDE, 128), F32),
             pltpu.VMEM((2, 2 * SIDE, 128), F32),
@@ -474,7 +502,7 @@
         rel_table,
         *lines,
     )
-    return merged.reshape(4, 12, 12, 1024)
+    return merged.reshape(12, 12, 4, 1024).transpose(2, 0, 1, 3)
 
 
 def solution(mesh):

time: 63.8 us -> 59.7 us (0.936)
  local copies, waits for them, and re-layouts: 5.99 us -> 2.79 us
  Pallas kernels: 57.6 us -> 56.1 us
    reshape x2 -> x0, local copies, waits for them, and re-layouts: 4.64 us -> none  [the longest x1 3.35 us: per_device(): return merged.reshape(4, 12, 12, 1024)]
    unnamed x0 -> x1, local copies, waits for them, and re-layouts: none -> 2.79 us
    pallas_call x1, Pallas kernels: 57.6 us -> 56.1 us  [per_device(): pl.pallas_call(functools.partial(kernel, *mesh_shape), out_shape=jax.Shap...]
    pad x1 -> x0, local copies, waits for them, and re-layouts: 1.35 us -> none  [per_device(): rel_table = jnp.pad(rel_table, ((0, 0), (0, 768 - rel_table.shape[1])))]
where the time goes in v2:
time: 59.7 us; the launch traced here: 58.9 us
  Pallas kernels  56.1 us (94%)
  local copies, waits for them, and re-layouts  2.79 us (5%)
    pallas_call x1, Pallas kernels, per_device(): pl.pallas_call(functools.partial(kernel, *mesh_shape), out_shape=jax.Shap...  56.1 us
    unnamed x1, local copies, waits for them, and re-layouts  2.79 us

profile of v2, /device:TPU:0, one launch (start us, length us, event | category | flops | bytes accessed | tf_op | source)
XLA Modules:
  0.0 58.9 jit_solution(17755897330994972842)
XLA Ops:
  0.0 56.1 %block.1 = bf16[144,4,1024]{2,1,0:T(4,128)(2,1)} custom-call(f32[2304,512]{1,0:T(8,128)} %bitcast.14, bf16[512,1536]{1,0:T(8,128)(2,1)} %qkv_weight.1, bf16[512,512]{1,0:T(8,128)(2,1)} %proj_weight.1, bf16[512,2048]{1,0:T(8,128)(2,1)} %fc1_weight.1, bf16[2048,512]{1,0:T(8,128)(2,1)} %fc2_weight.1, bf16[2048,1024]{1,0:T(8,128)(2,1)} %merge_weight.1, ...), custom_call_target="tpu_custom_call" | custom-call | tf_op jit(solution)/shard_map/block/pallas_call | solution.py:456
  56.1 2.8 %copy.21 = bf16[4,12,12,1024]{3,0,2,1:T(4,128)(2,1)} copy(bf16[4,12,12,1024]{3,0,2,1:T(4,128)(2,1)} %bitcast.13) | data formatting | bytes 2359296

commit v3 on v2

--- a/solution.py
+++ b/solution.py
@@ -28,10 +28,12 @@
 FROM = ((0, -1), (0, -1), (0, -1), (0, -1), (-1, 0), (-1, 0), (-1, -1))
 STEPS = (
     ((0, 1, 1), (0, 2, 1), (1, 0, 0), (1, 1, 0)),
-    ((0, 1, 0), (0, 2, 0), (0, 3, 0), (0, 0, 1)),
-    ((0, 0, 0), (1, 3, 1), (1, 0, 1), (1, 1, 1)),
-    ((1, 2, 1), (1, 3, 0), (0, 3, 1), (1, 2, 0)),
+    ((0, 1, 0), (0, 2, 0), (0, 3, 0), (1, 0, 1)),
+    ((0, 0, 0), (0, 0, 1), (1, 3, 1), (1, 3, 0)),
+    ((1, 1, 1), (1, 2, 1)),
+    ((0, 3, 1), (1, 2, 0)),
 )
+LOOPED = 3
 
 
 def segments(window):
@@ -141,25 +143,49 @@
         attended[pl.ds(first, WTOK), pl.ds(128 * pair, 128)] = jnp.where(left, results[0], results[1]).astype(BF16)
 
 
-def mark_window(ids, marks, window, first, lat, lat_count):
-    pair, wrow, wcol = window
-    row0, col0 = CORNER[pair][0] + 6 * wrow, CORNER[pair][1] + 12 * wcol
-    token = lax.broadcasted_iota(jnp.int32, (WTOK, 1), 0)
+def spread(spots):
+    token = lax.broadcasted_iota(jnp.int32, (WTOK, 128), 0)
     lev, row, col = token // 72, token // 12 % 6, token % 12
-    at_row = row0 + row
-    line = lev * SIDE + (at_row + SIDE) % SIDE
-    pick = lax.broadcasted_iota(jnp.int32, (WTOK, 2 * SIDE), 1) == line
-    rows = jnp.dot(jnp.where(pick, 1.0, 0.0).astype(BF16), ids[pair].astype(BF16), preferred_element_type=F32)
-    lane = lax.broadcasted_iota(jnp.int32, (WTOK, 128), 1)
-    region = jnp.sum(jnp.where(lane == (col0 + col + SIDE) % SIDE, rows, 0.0), -1, keepdims=True)
+    spots[0] = lev * SIDE + row
+    spots[1] = row
+    spots[2] = col
+
+
+def kinds(pair, regions, lat, lat_count):
+    line = lax.broadcasted_iota(jnp.int32, (2 * SIDE, 128), 0)
+    lev = jnp.where(line >= SIDE, 1, 0)
+    row = line - SIDE * lev
+    if pair == 0:
+        row = jnp.where(row >= SIDE - 3, row - SIDE, row)
+    else:
+        row = jnp.where(row < 3, row + SIDE, row)
     whole = lat_count * SIDE
-    orig = lat * SIDE + at_row
+    orig = lat * SIDE + row
     orig = jnp.where(orig < 0, orig + whole, jnp.where(orig >= whole, orig - whole, orig))
     band = jnp.where(orig >= whole - 3, 1, 0)
     if pair == 1:
         band = band + 2 * lev
-    kind = region.astype(jnp.int32) + 3 * band
-    marks[pl.ds(first, WTOK), :] = jnp.where(lane == kind, 1.0, 0.0).astype(BF16)
+    return regions + (3 * band + 1).astype(F32)
+
+
+def mark_window(ids, spots, marks, window, first):
+    pair, wrow, wcol = window
+    row0, col0 = CORNER[pair][0] + 6 * wrow, CORNER[pair][1] + 12 * wcol
+    line, row, col = spots[0] + row0, spots[1], spots[2] + col0
+    if row0 < 0:
+        line = jnp.where(row < -row0, line + SIDE, line)
+    elif row0 + 6 > SIDE:
+        line = jnp.where(row >= SIDE - row0, line - SIDE, line)
+    if col0 < 0:
+        col = jnp.where(col < 0, col + SIDE, col)
+    elif col0 + 12 > SIDE:
+        col = jnp.where(col >= SIDE, col - SIDE, col)
+    lane = lax.broadcasted_iota(jnp.int32, (WTOK, 128), 1)
+    pick = jnp.where(lane == line, 1.0, 0.0).astype(BF16)
+    rows = jnp.dot(pick, ids[pair].astype(BF16), preferred_element_type=F32)
+    own = jnp.where(lane == col, rows, 0.0).astype(BF16)
+    kind = jnp.dot(own, jnp.ones((128, 128), BF16), preferred_element_type=F32)
+    marks[pl.ds(first, WTOK), :] = jnp.where(lane.astype(F32) + 1.0 == kind, 1.0, 0.0).astype(BF16)
 
 
 def kernel(
@@ -204,6 +230,7 @@
     own_ids,
     far_ids,
     ids,
+    spots,
     halo_out,
     halo_in,
     back_out,
@@ -279,6 +306,7 @@
         )
 
     order = [slot for step in STEPS for slot in slots_of(step)]
+    late = slots_of(STEPS[LOOPED])
 
     for tile in range(TILES):
         token_load(tile).wait()
@@ -292,85 +320,134 @@
         for side in range(3):
             id_copy(pair, side).start()
     for pair, slot in order:
-        piece_copy(pair, slot, False).start()
-
-    ids[...] = own_ids[...]
+        if (pair, slot) not in late:
+            piece_copy(pair, slot, False).start()
+
+    ids[...] = jnp.zeros_like(ids)
+    for pair in range(2):
+        ids[pair, pl.ds(0, 2 * SIDE), :] = kinds(pair, own_ids[pair], lat, lat_count)
+    spread(spots)
     make_bias(rel_index, rel_table, table, bias)
 
     def all_ids():
         for pair in range(2):
             for side in range(3):
                 id_copy(pair, side).wait()
-            line = lax.broadcasted_iota(jnp.int32, (2 * SIDE, 128), 0) % SIDE
+            line = lax.broadcasted_iota(jnp.int32, (2 * SIDE, 128), 0)
+            line = jnp.where(line >= SIDE, line - SIDE, line)
             lane = lax.broadcasted_iota(jnp.int32, (2 * SIDE, 128), 1)
             far_row = line >= SIDE - 3 if pair == 0 else line < 3
             far_col = lane >= SIDE - 6 if pair == 0 else lane < 6
-            ids[pair] = jnp.where(
+            regions = jnp.where(
                 far_row,
                 jnp.where(far_col, far_ids[pair, 2], far_ids[pair, 1]),
                 jnp.where(far_col, far_ids[pair, 0], own_ids[pair]),
             )
+            ids[pair, pl.ds(0, 2 * SIDE), :] = kinds(pair, regions, lat, lat_count)
 
     for load in loads[:-1]:
         load.wait()
 
-    def run(step, _):
-        for number, windows in enumerate(STEPS):
-
-            @pl.when(step == number)
-            def _():
-                if number == 1:
-                    all_ids()
-                for pair, slot in slots_of(windows):
-                    piece_copy(pair, slot, False).wait_recv()
-                for place, window in enumerate(windows):
-                    for token, count, slot, first in segments(window):
-                        at = pl.ds(place * WTOK + token, count)
-                        if slot is None:
-                            part[:, at, :] = block[:, pl.ds(first, count), :]
-                        else:
-                            part[:, at, :] = halo_in[window[0], slot, :, pl.ds(first, count), :]
-                    mark_window(ids, marks, window, place * WTOK, lat, lat_count)
-
-        for place in range(G):
+    def first_norm(first, count):
+        for place in range(first, first + count):
             normed[pl.ds(place * WTOK, WTOK), :] = norm(
                 wide(part, place * WTOK, WTOK), norm1_gain[...], norm1_bias[...]
             ).astype(BF16)
+
+    def pack(first, count):
+        at = pl.ds(first * WTOK, count * WTOK)
         for third in range(3):
             columns = pl.ds(512 * third, 512)
-            packed = jnp.dot(normed[...], wq[:, columns], preferred_element_type=F32) + qkv_bias[columns].reshape(1, 512)
+            packed = jnp.dot(normed[at, :], wq[:, columns], preferred_element_type=F32)
+            packed = packed + qkv_bias[columns].reshape(1, 512)
             if third == 0:
                 packed = packed * 0.125
-            qkv[:, columns] = packed.astype(BF16)
-        for place in range(G):
+            qkv[at, columns] = packed.astype(BF16)
+
+    def project(first, count):
+        first, count = first * WTOK, count * WTOK
+        at = pl.ds(first, count)
+        hidden = jnp.dot(attended[at, :], wp[...], preferred_element_type=F32) + proj_bias[...]
+        hidden = hidden + wide(part, first, count)
+        put_wide(part, first, count, hidden)
+        normed[at, :] = norm(hidden, norm2_gain[...], norm2_bias[...]).astype(BF16)
+
+    def expand(first, count, quarter):
+        at = pl.ds(first * WTOK, count * WTOK)
+        columns = pl.ds(512 * quarter, 512)
+        units = jnp.dot(normed[at, :], w1[:, columns], preferred_element_type=F32) + fc1_bias[:, columns]
+        active[at, columns] = (0.5 * units * (1.0 + lax.erf(units * 0.7071067811865476))).astype(BF16)
+
+    def contract(first, count):
+        first, count = first * WTOK, count * WTOK
+        result = jnp.dot(active[pl.ds(first, count), :], w2[...], preferred_element_type=F32) + fc2_bias[...]
+        put_wide(part, first, count, result + wide(part, first, count))
+
+    def compute(count):
+        first_norm(0, count)
+        pack(0, count)
+        half = count // 2 if count > 2 else count
+        early = half + half // 2 if count > 2 else count
+        for place in range(early):
             attend(qkv, attended, bias, marks, place * WTOK)
-        hidden = jnp.dot(attended[...], wp[...], preferred_element_type=F32) + proj_bias[...] + wide(part, 0, ROWS)
-        put_wide(part, 0, ROWS, hidden)
-        normed[...] = norm(hidden, norm2_gain[...], norm2_bias[...]).astype(BF16)
+        project(0, half)
+        for place in range(early, count):
+            attend(qkv, attended, bias, marks, place * WTOK)
         for quarter in range(4):
-            columns = pl.ds(512 * quarter, 512)
-            units = jnp.dot(normed[...], w1[:, columns], preferred_element_type=F32) + fc1_bias[:, columns]
-            active[:, columns] = (0.5 * units * (1.0 + lax.erf(units * 0.7071067811865476))).astype(BF16)
-        result = jnp.dot(active[...], w2[...], preferred_element_type=F32) + fc2_bias[...] + wide(part, 0, ROWS)
-        put_wide(part, 0, ROWS, result)
-
-        for number, windows in enumerate(STEPS):
-
-            @pl.when(step == number)
-            def _():
-                for place, window in enumerate(windows):
-                    for token, count, slot, first in segments(window):
-                        at = pl.ds(place * WTOK + token, count)
-                        if slot is None:
-                            block[:, pl.ds(first, count), :] = part[:, at, :]
-                        else:
-                            back_out[window[0], slot, :, pl.ds(first, count), :] = part[:, at, :]
-                for pair, slot in slots_of(windows):
-                    piece_copy(pair, slot, True).start()
-
+            expand(0, half, quarter)
+        if half < count:
+            project(half, half)
+        contract(0, half)
+        if half < count:
+            for quarter in range(4):
+                expand(half, half, quarter)
+            contract(half, half)
+
+    def gather(number):
+        windows = STEPS[number]
+        if number == 1:
+            for pair, slot in late:
+                piece_copy(pair, slot, False).start()
+            all_ids()
+        for pair, slot in slots_of(windows):
+            piece_copy(pair, slot, False).wait_recv()
+        for place, window in enumerate(windows):
+            for token, count, slot, first in segments(window):
+                at = pl.ds(place * WTOK + token, count)
+                if slot is None:
+                    part[:, at, :] = block[:, pl.ds(first, count), :]
+                else:
+                    part[:, at, :] = halo_in[window[0], slot, :, pl.ds(first, count), :]
+            mark_window(ids, spots, marks, window, place * WTOK)
+
+    def settle(number):
+        windows = STEPS[number]
+        for place, window in enumerate(windows):
+            for token, count, slot, first in segments(window):
+                at = pl.ds(place * WTOK + token, count)
+                if slot is not None:
+                    back_out[window[0], slot, :, pl.ds(first, count), :] = part[:, at, :]
+        for pair, slot in slots_of(windows):
+            piece_copy(pair, slot, True).start()
+        for place, window in enumerate(windows):
+            for token, count, slot, first in segments(window):
+                at = pl.ds(place * WTOK + token, count)
+                if slot is None:
+                    block[:, pl.ds(first, count), :] = part[:, at, :]
+
+    def run(step, _):
+        for number in range(LOOPED):
+            pl.when(step == number)(functools.partial(gather, number))
+        compute(G)
+        for number in range(LOOPED):
+            pl.when(step == number)(functools.partial(settle, number))
         return 0
 
-    lax.fori_loop(0, len(STEPS), run, 0)
+    lax.fori_loop(0, LOOPED, run, 0)
+    for number in range(LOOPED, len(STEPS)):
+        gather(number)
+        compute(len(STEPS[number]))
+        settle(number)
 
     def merge(pair):
         for other, slot in order:
@@ -382,8 +459,8 @@
             loads[-1].wait()
 
         def merge_norm(step, _):
-            for number in range(4):
-                at = step * 4 + number
+            for number in range(8):
+                at = step * 8 + number
                 line = at + 12 if pair == 0 else lax.rem(at + 36, 48)
                 values = jnp.concatenate(
                     [
@@ -399,7 +476,7 @@
                 ).astype(BF16)
             return 0
 
-        lax.fori_loop(0, 6, merge_norm, 0)
+        lax.fori_loop(0, 3, merge_norm, 0)
         for quarter in range(4):
             merged = jnp.dot(normed3[...], wm[:, pl.ds(256 * quarter, 256)], preferred_element_type=F32)
             for at in range(24):
@@ -455,7 +532,7 @@
     vmem = pl.BlockSpec(memory_space=pltpu.VMEM)
     merged = pl.pallas_call(
         functools.partial(kernel, *mesh_shape),
-        out_shape=jax.ShapeDtypeStruct((144, 4, 1024), BF16),
+        out_shape=pltpu.VMEM((144, 4, 1024), BF16),
         in_specs=[hbm] * 6 + [vmem] * 13,
         out_specs=vmem,
         scratch_shapes=[
@@ -477,7 +554,8 @@
             pltpu.VMEM((8, 768), F32),
             pltpu.VMEM((2, 2 * SIDE, 128), F32),
             pltpu.VMEM((2, 3, 2 * SIDE, 128), F32),
-            pltpu.VMEM((2, 2 * SIDE, 128), F32),
+            pltpu.VMEM((2, 128, 128), F32),
+            pltpu.VMEM((3, WTOK, 128), jnp.int32),
         ]
         + [pltpu.VMEM((2, 7, TILES, SLOT, 128), F32)] * 4
         + [

time: 59.7 us -> 56.4 us (0.945)
  the two profiles are of different devices: /device:TPU:0 before, /device:TPU:24 now
where the time goes in v3:
time: 56.4 us; the launch traced here: 56.3 us
  Pallas kernels  55.3 us (98%)
  local copies, waits for them, and re-layouts  1.02 us (2%)
    pallas_call x1, Pallas kernels, per_device(): pl.pallas_call(functools.partial(kernel, *mesh_shape), out_shape=pltpu.VM...  55.3 us

profile of v3, /device:TPU:24, one launch (start us, length us, event | category | flops | bytes accessed | tf_op | source)
XLA Modules:
  0.0 56.3 jit_solution(10035040428175399723)
XLA Ops:
  0.0 55.3 %block.1 = bf16[144,4,1024]{2,1,0:T(4,128)(2,1)S(1)} custom-call(f32[2304,512]{1,0:T(8,128)} %bitcast.14, bf16[512,1536]{1,0:T(8,128)(2,1)} %qkv_weight.1, bf16[512,512]{1,0:T(8,128)(2,1)} %proj_weight.1, bf16[512,2048]{1,0:T(8,128)(2,1)} %fc1_weight.1, bf16[2048,512]{1,0:T(8,128)(2,1)} %fc2_weight.1, bf16[2048,1024]{1,0:T(8,128)(2,1)} %merge_weight.1, ...), custom_call_target="tpu_custom_call" | custom-call | tf_op jit(solution)/shard_map/block/pallas_call | solution.py:533
  55.3 1.0 %copy.21 = bf16[4,12,12,1024]{3,0,2,1:T(4,128)(2,1)} copy(bf16[4,12,12,1024]{3,0,2,1:T(4,128)(2,1)S(1)} %bitcast.13) | data formatting | bytes 2359296

commit v4 on v3

--- a/solution.py
+++ b/solution.py
@@ -29,11 +29,13 @@
 STEPS = (
     ((0, 1, 1), (0, 2, 1), (1, 0, 0), (1, 1, 0)),
     ((0, 1, 0), (0, 2, 0), (0, 3, 0), (1, 0, 1)),
+    ((1, 1, 1), (1, 2, 1)),
     ((0, 0, 0), (0, 0, 1), (1, 3, 1), (1, 3, 0)),
-    ((1, 1, 1), (1, 2, 1)),
     ((0, 3, 1), (1, 2, 0)),
 )
-LOOPED = 3
+LOOPED = (0, 1, 3)
+BETWEEN, LAST = 2, 4
+LINES = (tuple(range(2, 10)), (0, 1, 10, 11))
 
 
 def segments(window):
@@ -306,7 +308,7 @@
         )
 
     order = [slot for step in STEPS for slot in slots_of(step)]
-    late = slots_of(STEPS[LOOPED])
+    late = slots_of(STEPS[BETWEEN])
 
     for tile in range(TILES):
         token_load(tile).wait()
@@ -435,33 +437,38 @@
                 if slot is None:
                     block[:, pl.ds(first, count), :] = part[:, at, :]
 
-    def run(step, _):
-        for number in range(LOOPED):
-            pl.when(step == number)(functools.partial(gather, number))
-        compute(G)
-        for number in range(LOOPED):
-            pl.when(step == number)(functools.partial(settle, number))
-        return 0
-
-    lax.fori_loop(0, LOOPED, run, 0)
-    for number in range(LOOPED, len(STEPS)):
+    def short(number):
         gather(number)
         compute(len(STEPS[number]))
         settle(number)
 
-    def merge(pair):
-        for other, slot in order:
-            if other == pair:
+    def run(step, _):
+        for at, number in enumerate(LOOPED):
+            if at == 2:
+                pl.when(step == at)(functools.partial(short, BETWEEN))
+            pl.when(step == at)(functools.partial(gather, number))
+        compute(G)
+        for at, number in enumerate(LOOPED):
+            pl.when(step == at)(functools.partial(settle, number))
+        return 0
+
+    lax.fori_loop(0, len(LOOPED), run, 0)
+    short(LAST)
+
+    def merge(part_of, rows):
+        for pair, slot in order:
+            if (slot > 2) == (part_of == 1):
                 piece_copy(pair, slot, True).wait_recv()
                 for first, count, where in piece_runs(pair, slot):
                     block[:, pl.ds(where, count), :] = back_in[pair, slot, :, pl.ds(first, count), :]
-        if pair == 0:
+        if part_of == 0:
             loads[-1].wait()
+        levels = 8 // len(rows)
 
         def merge_norm(step, _):
             for number in range(8):
                 at = step * 8 + number
-                line = at + 12 if pair == 0 else lax.rem(at + 36, 48)
+                line = (step * levels + number // len(rows)) * 12 + rows[number % len(rows)]
                 values = jnp.concatenate(
                     [
                         block[tile, pl.ds(line * 2 * SIDE + row * SIDE + col, 16, stride=2), :]
@@ -476,17 +483,22 @@
                 ).astype(BF16)
             return 0
 
-        lax.fori_loop(0, 3, merge_norm, 0)
+        lax.fori_loop(0, 4 // levels, merge_norm, 0)
         for quarter in range(4):
-            merged = jnp.dot(normed3[...], wm[:, pl.ds(256 * quarter, 256)], preferred_element_type=F32)
-            for at in range(24):
+            merged = jnp.dot(
+                normed3[pl.ds(0, 64 * len(rows)), :],
+                wm[:, pl.ds(256 * quarter, 256)],
+                preferred_element_type=F32,
+            )
+            for at in range(4 * len(rows)):
+                first = rows[at % len(rows)] * 48 + at // len(rows)
                 for half in range(2):
-                    product[
-                        2 * quarter + half, pl.ds(at % 12 * 48 + LEVELS[pair][at // 12], 12, stride=4), :
-                    ] = merged[16 * at : 16 * at + 12, 128 * half : 128 * (half + 1)]
-
-    merge(0)
-    merge(1)
+                    product[2 * quarter + half, pl.ds(first, 12, stride=4), :] = merged[
+                        16 * at : 16 * at + 12, 128 * half : 128 * (half + 1)
+                    ]
+
+    for part_of, rows in enumerate(LINES):
+        merge(part_of, rows)
     for tile in range(8):
         out[:, :, pl.ds(128 * tile, 128)] = product[tile].astype(BF16).reshape(144, 4, 128)
 
@@ -549,7 +561,7 @@
             pltpu.VMEM((ROWS, 1536), BF16),
             pltpu.VMEM((ROWS, 512), BF16),
             pltpu.VMEM((ROWS, 2048), BF16),
-            pltpu.VMEM((384, 2048), BF16),
+            pltpu.VMEM((512, 2048), BF16),
             pltpu.VMEM((8, 576, 128), F32),
             pltpu.VMEM((8, 768), F32),
             pltpu.VMEM((2, 2 * SIDE, 128), F32),

time: 56.4 us -> 55.1 us (0.977)
  the two profiles are of different devices: /device:TPU:24 before, /device:TPU:0 now
where the time goes in v4:
time: 55.1 us; the launch traced here: 55 us
  Pallas kernels  54 us (98%)
  local copies, waits for them, and re-layouts  1.02 us (2%)
    pallas_call x1, Pallas kernels, per_device(): pl.pallas_call(functools.partial(kernel, *mesh_shape), out_shape=pltpu.VM...  54 us

profile of v4, /device:TPU:0, one launch (start us, length us, event | category | flops | bytes accessed | tf_op | source)
XLA Modules:
  0.0 55.0 jit_solution(2728925938910677716)
XLA Ops:
  0.0 54.0 %block.1 = bf16[144,4,1024]{2,1,0:T(4,128)(2,1)S(1)} custom-call(f32[2304,512]{1,0:T(8,128)} %bitcast.14, bf16[512,1536]{1,0:T(8,128)(2,1)} %qkv_weight.1, bf16[512,512]{1,0:T(8,128)(2,1)} %proj_weight.1, bf16[512,2048]{1,0:T(8,128)(2,1)} %fc1_weight.1, bf16[2048,512]{1,0:T(8,128)(2,1)} %fc2_weight.1, bf16[2048,1024]{1,0:T(8,128)(2,1)} %merge_weight.1, ...), custom_call_target="tpu_custom_call" | custom-call | tf_op jit(solution)/shard_map/block/pallas_call | solution.py:545
  54.0 1.0 %copy.21 = bf16[4,12,12,1024]{3,0,2,1:T(4,128)(2,1)} copy(bf16[4,12,12,1024]{3,0,2,1:T(4,128)(2,1)S(1)} %bitcast.13) | data formatting | bytes 2359296

commit v5 on v4

--- a/solution.py
+++ b/solution.py
@@ -308,7 +308,7 @@
         )
 
     order = [slot for step in STEPS for slot in slots_of(step)]
-    late = slots_of(STEPS[BETWEEN])
+    late = slots_of(STEPS[LOOPED[2]])
 
     for tile in range(TILES):
         token_load(tile).wait()

time: 55.1 us -> 52.8 us (0.958)
  Pallas kernels: 54 us -> 51.4 us
    pallas_call x1, Pallas kernels: 54 us -> 51.4 us  [per_device(): pl.pallas_call(functools.partial(kernel, *mesh_shape), out_shape=pltpu.VM...]
where the time goes in v5:
time: 52.8 us; the launch traced here: 52.4 us
  Pallas kernels  51.4 us (97%)
  local copies, waits for them, and re-layouts  1.02 us (2%)
    pallas_call x1, Pallas kernels, per_device(): pl.pallas_call(functools.partial(kernel, *mesh_shape), out_shape=pltpu.VM...  51.4 us

profile of v5, /device:TPU:0, one launch (start us, length us, event | category | flops | bytes accessed | tf_op | source)
XLA Modules:
  0.0 52.4 jit_solution(13468668897263577958)
XLA Ops:
  0.0 51.4 %block.1 = bf16[144,4,1024]{2,1,0:T(4,128)(2,1)S(1)} custom-call(f32[2304,512]{1,0:T(8,128)} %bitcast.14, bf16[512,1536]{1,0:T(8,128)(2,1)} %qkv_weight.1, bf16[512,512]{1,0:T(8,128)(2,1)} %proj_weight.1, bf16[512,2048]{1,0:T(8,128)(2,1)} %fc1_weight.1, bf16[2048,512]{1,0:T(8,128)(2,1)} %fc2_weight.1, bf16[2048,1024]{1,0:T(8,128)(2,1)} %merge_weight.1, ...), custom_call_target="tpu_custom_call" | custom-call | tf_op jit(solution)/shard_map/block/pallas_call | solution.py:545
  51.4 1.0 %copy.21 = bf16[4,12,12,1024]{3,0,2,1:T(4,128)(2,1)} copy(bf16[4,12,12,1024]{3,0,2,1:T(4,128)(2,1)S(1)} %bitcast.13) | data formatting | bytes 2359296

commit v6 on v5

--- a/solution.py
+++ b/solution.py
@@ -314,16 +314,20 @@
         token_load(tile).wait()
     for load in loads:
         load.start()
-    for pair, slot in order:
-        for first, count, where in piece_runs(pair, slot):
-            halo_out[pair, slot, :, pl.ds(first, count), :] = block[:, pl.ds(where, count), :]
+    def fill(pieces):
+        for pair, slot in pieces:
+            for first, count, where in piece_runs(pair, slot):
+                halo_out[pair, slot, :, pl.ds(first, count), :] = block[:, pl.ds(where, count), :]
+
+    soon = [piece for piece in order if piece not in late]
+    fill(soon)
     pl.semaphore_wait(barrier, len(around))
+    for pair, slot in soon:
+        piece_copy(pair, slot, False).start()
     for pair in range(2):
         for side in range(3):
             id_copy(pair, side).start()
-    for pair, slot in order:
-        if (pair, slot) not in late:
-            piece_copy(pair, slot, False).start()
+    fill(late)
 
     ids[...] = jnp.zeros_like(ids)
     for pair in range(2):

time: 52.8 us -> 54.8 us (1.038)
  Pallas kernels: 51.4 us -> 53 us
    pallas_call x1, Pallas kernels: 51.4 us -> 53 us  [per_device(): pl.pallas_call(functools.partial(kernel, *mesh_shape), out_shape=pltpu.VM...]
where the time goes in v6:
time: 54.8 us; the launch traced here: 54 us
  Pallas kernels  53 us (97%)
  local copies, waits for them, and re-layouts  1.02 us (2%)
    pallas_call x1, Pallas kernels, per_device(): pl.pallas_call(functools.partial(kernel, *mesh_shape), out_shape=pltpu.VM...  53 us

profile of v6, /device:TPU:0, one launch (start us, length us, event | category | flops | bytes accessed | tf_op | source)
XLA Modules:
  0.0 54.0 jit_solution(4018155888713982557)
XLA Ops:
  0.0 53.0 %block.1 = bf16[144,4,1024]{2,1,0:T(4,128)(2,1)S(1)} custom-call(f32[2304,512]{1,0:T(8,128)} %bitcast.14, bf16[512,1536]{1,0:T(8,128)(2,1)} %qkv_weight.1, bf16[512,512]{1,0:T(8,128)(2,1)} %proj_weight.1, bf16[512,2048]{1,0:T(8,128)(2,1)} %fc1_weight.1, bf16[2048,512]{1,0:T(8,128)(2,1)} %fc2_weight.1, bf16[2048,1024]{1,0:T(8,128)(2,1)} %merge_weight.1, ...), custom_call_target="tpu_custom_call" | custom-call | tf_op jit(solution)/shard_map/block/pallas_call | solution.py:549
  53.0 1.0 %copy.21 = bf16[4,12,12,1024]{3,0,2,1:T(4,128)(2,1)} copy(bf16[4,12,12,1024]{3,0,2,1:T(4,128)(2,1)S(1)} %bitcast.13) | data formatting | bytes 2359296
